TPU v7x, 512 devices: a whole 4x4x16 slice. The times are simulated.
512 devices in a mesh: seq: 32 (over x, z_lo), head: 8 (over y, core), enc: 2 (over z_hi).
Axes of the slice: x: 4, y: 4, z: 16 (z_hi: 2, z_lo: 8; z = z_hi * 8 + z_lo), core: 2. Of those that a mesh axis runs over, the one named last changes fastest.
Arguments:
- queries: bfloat16 [10240, 4096], P('seq', ('head', 'enc')), may hold values from -2000 to 2000
- keys: bfloat16 [10240, 4096], P('seq', ('head', 'enc')), may hold values from -2000 to 2000
- values: bfloat16 [10240, 4096], P('seq', ('head', 'enc')), may hold values from -6 to 6
- out_weight: bfloat16 [4096, 5120], P(('head', 'enc'), 'seq'), may hold values from -0.1875 to 0.1875
- q_gain: float32 [4096], P(('head', 'enc')), may hold values from 0.75 to 3
- k_gain: float32 [4096], P(('head', 'enc')), may hold values from 0.75 to 3
- gate: float32 [5120], P(('head', 'enc')), may hold values from 1 to 8
- valid_count: int32 [1], replicated, may hold values from 5120 to 10240
Outputs:
- update: bfloat16 [10240, 5120], P('seq', ('head', 'enc'))
Inputs may be any that keep to these rules, and one draw needn't show every extreme that they name: Key positions from valid_count[0] on are padding and take no weight.
All inputs are finite; a program needn't handle non-finite values.
Results may differ from a plain program's by a relative error of at most 0.015.
The roundings to bfloat16 on the way count: a program that leaves them out, or rounds other values in their place, can miss the bound.
Values may be sent and summed in bfloat16 or wider, within the bound.
No kernel may reach another device: no remote copies, remote signals or barrier semaphores. Data moves between devices by JAX's collectives and lax.ppermute only.
A program may use at most 64 MiB of HBM per device.

v0:
```python
import jax
import jax.numpy as jnp
from jax import lax
from jax.sharding import PartitionSpec as P

HEAD_DIM = 128
epsilon = 1e-06
lowest_score = -1e30


def normalize(matrix, squares, gain_row, feature_count):
    inverse_rms = lax.rsqrt(squares / feature_count + epsilon)
    return (matrix.astype(jnp.float32) * inverse_rms[:, None] * gain_row[None, :]).astype(
        jnp.bfloat16
    )


def absorb(carried, query_heads, key_block, value_block, offset, key_limit):
    running_sum, running_max, running_mass = carried
    scale_factor = query_heads.shape[2] ** (-0.5)
    scores = (
        jnp.einsum("qhd,khd->hqk", query_heads, key_block, preferred_element_type=jnp.float32)
        * scale_factor
    )
    position = offset + jnp.arange(key_block.shape[0], dtype=jnp.int32)
    usable = (position < key_limit)[None, None, :]
    masked = jnp.where(usable, scores, lowest_score)
    new_max = jnp.maximum(running_max, jnp.max(masked, axis=2))
    weights = jnp.where(usable, jnp.exp(masked - new_max[:, :, None]), 0.0)
    factor = jnp.exp(running_max - new_max)
    running_mass = running_mass * factor + jnp.sum(weights, axis=2)
    running_sum = running_sum * factor[:, :, None] + jnp.einsum(
        "hqk,khd->hqd",
        weights.astype(jnp.bfloat16),
        value_block,
        preferred_element_type=jnp.float32,
    )
    return (running_sum, new_max, running_mass)


def absorb_blocks(carried, query_heads, key_rows, value_rows, key_limit):
    row_total = key_rows.shape[0]
    block_size = 512
    block_count = row_total // block_size
    key_blocks = key_rows.reshape((block_count, block_size) + key_rows.shape[1:])
    value_blocks = value_rows.reshape((block_count, block_size) + value_rows.shape[1:])

    def absorb_block(running, triple):
        block_number, key_block, value_block = triple
        return (
            absorb(
                running, query_heads, key_block, value_block, block_number * block_size, key_limit
            ),
            None,
        )

    numbers = jnp.arange(block_count, dtype=jnp.int32)
    carried, _ = lax.scan(absorb_block, carried, (numbers, key_blocks, value_blocks))
    return carried


def visit(carried, query_heads, key_rows, value_rows, key_limit):
    return absorb_blocks(carried, query_heads, key_rows, value_rows, key_limit)


def local(queries, keys, values, out_weight, q_gain, k_gain, gate, valid_count):
    row_count = queries.shape[0]
    local_heads = queries.shape[1] // HEAD_DIM
    feature_count = queries.shape[1] * lax.axis_size(("head", "enc"))
    key_limit = valid_count[0]
    query_squares = jnp.sum(jnp.square(queries.astype(jnp.float32)), axis=1)
    key_squares = jnp.sum(jnp.square(keys.astype(jnp.float32)), axis=1)
    query_totals, key_totals = lax.psum((query_squares, key_squares), ("head", "enc"))
    query_heads = normalize(queries, query_totals, q_gain, feature_count).reshape(
        row_count, local_heads, HEAD_DIM
    )
    key_heads = normalize(keys, key_totals, k_gain, feature_count).reshape(
        row_count, local_heads, HEAD_DIM
    )
    value_heads = values.reshape(row_count, local_heads, HEAD_DIM)
    initial = (
        jnp.zeros((local_heads, row_count, HEAD_DIM), jnp.float32),
        jnp.full((local_heads, row_count), lowest_score, jnp.float32),
        jnp.zeros((local_heads, row_count), jnp.float32),
    )
    running_sum, running_max, running_mass = visit(
        initial,
        query_heads,
        lax.all_gather(key_heads, "seq", axis=0, tiled=True),
        lax.all_gather(value_heads, "seq", axis=0, tiled=True),
        key_limit,
    )
    attended = (running_sum / running_mass[:, :, None]).transpose(1, 0, 2)
    attended = attended.reshape(row_count, local_heads * HEAD_DIM).astype(jnp.bfloat16)
    terms = jnp.dot(
        attended,
        lax.all_gather(out_weight, "seq", axis=1, tiled=True),
        preferred_element_type=jnp.float32,
    )
    summed = lax.psum_scatter(
        terms.astype(jnp.bfloat16), ("head", "enc"), scatter_dimension=1, tiled=True
    ).astype(jnp.float32)
    return (gate[None, :] * summed).astype(jnp.bfloat16)


def solution(mesh):
    placed = (
        P("seq", ("head", "enc")),
        P("seq", ("head", "enc")),
        P("seq", ("head", "enc")),
        P(("head", "enc"), "seq"),
        P(("head", "enc")),
        P(("head", "enc")),
        P(("head", "enc")),
        P(),
    )
    return jax.shard_map(
        local, mesh=mesh, in_specs=placed, out_specs=P("seq", ("head", "enc")), check_vma=False
    )
```

profile of v0, /device:TPU:2, one launch (start us, length us, event | category | flops | bytes accessed | tf_op | source)
XLA Modules:
  0.0 957.6 jit_solution(13073559487828346287)
XLA Ops:
  6.5 1.1 fusion.11
  7.6 1.1 fusion.14
  8.7 78.0 %all-reduce = (f32[320]{0:T(512)S(1)}, f32[320]{0:T(512)S(1)}) all-reduce(f32[320]{0:T(512)S(1)} %fusion.11, f32[320]{0:T(512)S(1)} %fusion.14), channel_id=1, replica_groups=mesh['seq'=32,'head'=8,'enc'=2] {'head','enc'}, use_global_device_ids=true, to_apply=%region_1.0 | all-reduce | flops 640 | bytes 5120 | tf_op jit(solution)/shard_map/psum | solution.py:73
  88.5 1.6 reshape.35
  91.1 214.0 %all-gather.4.cloned.1.call-done = bf16[10240,2,128]{2,1,0:T(2,128)(2,1)} async-done(((bf16[320,2,128]{2,1,0:T(2,128)(2,1)}), bf16[10240,2,128]{2,1,0:T(2,128)(2,1)}) %all-gather.4.cloned.1.call-update) | async-done | bytes 5242896 | tf_op jit(solution)/shard_map/all_gather | solution.py:89
  305.2 242.4 %all-gather.6.cloned.1.call-done = bf16[10240,2,128]{2,1,0:T(2,128)(2,1)} async-done(((bf16[320,2,128]{2,1,0:T(2,128)(2,1)}), bf16[10240,2,128]{2,1,0:T(2,128)(2,1)}) %all-gather.6.cloned.1.call-update) | async-done | bytes 5242896 | tf_op jit(solution)/shard_map/all_gather | solution.py:90
  547.6 92.4 %while.15 = (s32[]{:T(128)}, f32[2,320,128]{2,1,0:T(8,128)S(1)}, f32[2,320]{1,0:T(2,128)S(1)}, f32[2,320]{1,0:T(2,128)S(1)}, s32[20]{0:T(128)S(1)}, /*index=5*/s...) while((s32[]{:T(128)}, f32[2,320,128]{2,1,0:T(8,128)S(1)}, ...), condition=%wide.region_7.8_spmd.clone, body=%wide.region_4.7_spmd.clone.sunk | while | flops 170971264 | bytes 6367397 | solution.py:58
  549.4 1.4 constant_dynamic-slice_fusion.3
  554.1 1.4 constant_dynamic-slice_fusion.3
  558.7 1.4 constant_dynamic-slice_fusion.3
  563.3 1.4 constant_dynamic-slice_fusion.3
  567.9 1.4 constant_dynamic-slice_fusion.3
  572.6 1.4 constant_dynamic-slice_fusion.3
  577.2 1.4 constant_dynamic-slice_fusion.3
  581.8 1.4 constant_dynamic-slice_fusion.3
  586.4 1.4 constant_dynamic-slice_fusion.3
  591.1 1.4 constant_dynamic-slice_fusion.3
  595.7 1.4 constant_dynamic-slice_fusion.3
  600.3 1.4 constant_dynamic-slice_fusion.3
  604.9 1.4 constant_dynamic-slice_fusion.3
  609.5 1.4 constant_dynamic-slice_fusion.3
  614.2 1.4 constant_dynamic-slice_fusion.3
  618.8 1.4 constant_dynamic-slice_fusion.3
  623.4 1.4 constant_dynamic-slice_fusion.3
  628.0 1.4 constant_dynamic-slice_fusion.3
  632.7 1.4 constant_dynamic-slice_fusion.3
  637.3 1.4 constant_dynamic-slice_fusion.3
  640.0 136.6 %all-gather.8.cloned.1.call-done = bf16[256,5120]{0,1:T(8,128)(2,1)} async-done(((bf16[256,160]{0,1:T(8,128)(2,1)}), bf16[256,5120]{0,1:T(8,128)(2,1)}) %all-gather.8.cloned.1.call-update) | async-done | bytes 2621456 | tf_op jit(solution)/shard_map/all_gather | solution.py:97
  776.6 2.9 convolution_convert_fusion
  779.6 3.6 copy.29
  783.2 166.0 %reduce-scatter.4.cloned.1.call-done = bf16[320,320]{1,0:T(8,128)(2,1)} async-done(((bf16[5120,320]{1,0:T(8,128)(2,1)}), bf16[320,320]{1,0:T(8,128)(2,1)}) %reduce-scatter.4.cloned.1.call-update) | async-done | bytes 204816
  949.2 1.1 copy.30
  (185 shorter events, 53.9 us)
Async XLA Ops:
  6.5 84.5 %copy-start.1 = (bf16[320,256]{1,0:T(8,128)(2,1)S(1)}, bf16[320,256]{1,0:T(8,128)(2,1)}, u32[]{:S(2)}) copy-start(bf16[320,256]{1,0:T(8,128)(2,1)} %param.10) | copy-start | bytes 491524
  6.5 84.5 %copy-start.3 = (f32[256]{0:T(256)S(1)}, f32[256]{0:T(256)}, u32[]{:S(2)}) copy-start(f32[256]{0:T(256)} %param.14) | copy-start | bytes 3076
  6.5 298.6 %all-gather.4.cloned.1.call-start = ((), (), s32[]{:S(2)}) async-start(), calls=%async_computation.1 | async-start | bytes 5406720 | tf_op jit(solution)/shard_map/all_gather | solution.py:89
  88.5 459.1 %all-gather.6.cloned.1.call-start = ((), (), s32[]{:S(2)}) async-start(), calls=%async_computation.2 | async-start | bytes 5406720 | tf_op jit(solution)/shard_map/all_gather | solution.py:90
  90.2 686.4 %all-gather.8.cloned.1.call-start = ((), (), s32[]{:S(2)}) async-start(), calls=%async_computation.3 | async-start | bytes 2703360 | tf_op jit(solution)/shard_map/all_gather | solution.py:97
  90.9 858.3 %reduce-scatter.4.cloned.1.call-start = ((), (), s32[]{:S(2)}) async-start(), calls=%async_computation.4 | async-start | bytes 4177920
  640.0 136.6 %copy-start = (f32[2,320,128]{2,1,0:T(8,128)}, f32[2,320,128]{2,1,0:T(8,128)S(1)}, u32[]{:S(2)}) copy-start(f32[2,320,128]{2,1,0:T(8,128)S(1)} %get-tuple-element.53) | copy-start | bytes 983044
  783.2 167.2 %copy-start.2 = (f32[320]{0:T(512)S(1)}, f32[320]{0:T(512)}, u32[]{:S(2)}) copy-start(f32[320]{0:T(512)} %param.16) | copy-start | bytes 3844
Sparse Core Ops, SparseCore 0:
  88.6 216.5 all-gather.3
  307.2 240.2 all-gather.5
  549.6 226.9 all-gather.7
  783.4 165.8 reduce-scatter.3
where the time goes:
time: 959 us; the launch traced here: 958 us
  waiting for transfers between devices  760 us (79%)
  blocking collectives  78 us (8%)
  local copies, waits for them, and re-layouts  46.8 us (5%)
  other arithmetic  25.5 us (3%)
  matrix products  20.2 us (2%)
  loops' own time  14.1 us (1%)
  between operations  13.2 us (1%)
    all_gather x1, waiting for transfers between devices, local(): lax.all_gather(value_heads, 'seq', axis=0, tiled=True)  242 us
    all_gather x1, waiting for transfers between devices, local(): lax.all_gather(key_heads, 'seq', axis=0, tiled=True)  214 us
    unnamed x5, waiting for transfers between devices  167 us
    all_gather x1, waiting for transfers between devices, local(): lax.all_gather(out_weight, 'seq', axis=1, tiled=True)  137 us
    psum x1, blocking collectives, local(): lax.psum((query_squares, key_squares), ('head', 'enc'))  78 us
    dynamic_slice x40, local copies, waits for them, and re-layouts, absorb_blocks(): lax.scan(absorb_block, carried, (numbers, key_blocks, value_blocks))  39.7 us
  transfers between devices with their start and end apart: 4, of which 4 were waited for; matrix products, arithmetic and copies ran while one was open for 8% of the time, Pallas kernels for 0%

commit v1 on v0

--- a/solution.py
+++ b/solution.py
@@ -6,6 +6,10 @@
 HEAD_DIM = 128
 epsilon = 1e-06
 lowest_score = -1e30
+
+
+def pass_shards(arr_in, row_axis, axis_tag):
+    return lax.psum(lax.psum(arr_in, row_axis), axis_tag)
 
 
 def normalize(matrix, squares, gain_row, feature_count):
@@ -70,7 +74,7 @@
     key_limit = valid_count[0]
     query_squares = jnp.sum(jnp.square(queries.astype(jnp.float32)), axis=1)
     key_squares = jnp.sum(jnp.square(keys.astype(jnp.float32)), axis=1)
-    query_totals, key_totals = lax.psum((query_squares, key_squares), ("head", "enc"))
+    query_totals, key_totals = pass_shards((query_squares, key_squares), "enc", "head")
     query_heads = normalize(queries, query_totals, q_gain, feature_count).reshape(
         row_count, local_heads, HEAD_DIM
     )

time: 959 us -> 917 us (0.956)
  blocking collectives: 78 us -> 30.7 us
    psum x1 -> x2, blocking collectives: 78 us -> 30.7 us  [pass_shards(): return lax.psum(lax.psum(arr_in, row_axis), axis_tag)]
  transfers between devices with their start and end apart: 4 -> 4, of which waited for: 4 -> 4; matrix products, arithmetic and copies ran while one was open for 8% -> 9% of each run, Pallas kernels for 0% -> 0%
where the time goes in v1:
time: 917 us; the launch traced here: 916 us
  waiting for transfers between devices  767 us (84%)
  local copies, waits for them, and re-layouts  46.8 us (5%)
  blocking collectives  30.7 us (3%)
  other arithmetic  24.5 us (3%)
  matrix products  20.2 us (2%)
  loops' own time  14.1 us (2%)
  between operations  13.2 us (1%)
    all_gather x1, waiting for transfers between devices, local(): lax.all_gather(value_heads, 'seq', axis=0, tiled=True)  242 us
    all_gather x1, waiting for transfers between devices, local(): lax.all_gather(key_heads, 'seq', axis=0, tiled=True)  221 us
    unnamed x5, waiting for transfers between devices  167 us
    all_gather x1, waiting for transfers between devices, local(): lax.all_gather(out_weight, 'seq', axis=1, tiled=True)  137 us
    dynamic_slice x40, local copies, waits for them, and re-layouts, absorb_blocks(): lax.scan(absorb_block, carried, (numbers, key_blocks, value_blocks))  39.7 us
    psum x2, blocking collectives, pass_shards(): return lax.psum(lax.psum(arr_in, row_axis), axis_tag)  30.7 us
  transfers between devices with their start and end apart: 4, of which 4 were waited for; matrix products, arithmetic and copies ran while one was open for 9% of the time, Pallas kernels for 0%

profile of v1, /device:TPU:2, one launch (start us, length us, event | category | flops | bytes accessed | tf_op | source)
XLA Modules:
  0.0 916.4 jit_solution(7844708087662312824)
XLA Ops:
  6.5 1.2 fusion.11
  7.8 16.7 %all-reduce.1 = (f32[320]{0:T(512)S(1)}, f32[320]{0:T(512)S(1)}) all-reduce(f32[320]{0:T(512)S(1)} %get-tuple-element.140, f32[320]{0:T(512)S(1)} %get-tuple-element.141), channel_id=1, replica_groups=mesh['seq'=32,'head'=8,'enc'=2] {'enc'}, use_global_device_ids=true, to_apply=%region_1.0 | all-reduce | flops 640 | bytes 5120 | tf_op jit(solution)/shard_map/psum | solution.py:12
  24.5 14.0 %all-reduce = (f32[320]{0:T(512)S(1)}, f32[320]{0:T(512)S(1)}) all-reduce(f32[320]{0:T(512)S(1)} %get-tuple-element.132, f32[320]{0:T(512)S(1)} %get-tuple-element.133), channel_id=1, replica_groups=mesh['seq'=32,'head'=8,'enc'=2] {'head'}, use_global_device_ids=true, to_apply=%region_2.0 | all-reduce | flops 640 | bytes 5120 | tf_op jit(solution)/shard_map/psum | solution.py:12
  40.3 1.6 reshape.35
  42.9 220.9 %all-gather.4.cloned.1.call-done = bf16[10240,2,128]{2,1,0:T(2,128)(2,1)} async-done(((bf16[320,2,128]{2,1,0:T(2,128)(2,1)}), bf16[10240,2,128]{2,1,0:T(2,128)(2,1)}) %all-gather.4.cloned.1.call-update) | async-done | bytes 5242896 | tf_op jit(solution)/shard_map/all_gather | solution.py:93
  263.8 242.4 %all-gather.6.cloned.1.call-done = bf16[10240,2,128]{2,1,0:T(2,128)(2,1)} async-done(((bf16[320,2,128]{2,1,0:T(2,128)(2,1)}), bf16[10240,2,128]{2,1,0:T(2,128)(2,1)}) %all-gather.6.cloned.1.call-update) | async-done | bytes 5242896 | tf_op jit(solution)/shard_map/all_gather | solution.py:94
  506.2 92.4 %while.15 = (s32[]{:T(128)}, f32[2,320,128]{2,1,0:T(8,128)S(1)}, f32[2,320]{1,0:T(2,128)S(1)}, f32[2,320]{1,0:T(2,128)S(1)}, s32[20]{0:T(128)S(1)}, /*index=5*/s...) while((s32[]{:T(128)}, f32[2,320,128]{2,1,0:T(8,128)S(1)}, ...), condition=%wide.region_9.10_spmd.clone, body=%wide.region_6.9_spmd.clone.sunk | while | flops 170971264 | bytes 6367397 | solution.py:62
  508.1 1.4 constant_dynamic-slice_fusion.3
  512.7 1.4 constant_dynamic-slice_fusion.3
  517.3 1.4 constant_dynamic-slice_fusion.3
  521.9 1.4 constant_dynamic-slice_fusion.3
  526.6 1.4 constant_dynamic-slice_fusion.3
  531.2 1.4 constant_dynamic-slice_fusion.3
  535.8 1.4 constant_dynamic-slice_fusion.3
  540.4 1.4 constant_dynamic-slice_fusion.3
  545.1 1.4 constant_dynamic-slice_fusion.3
  549.7 1.4 constant_dynamic-slice_fusion.3
  554.3 1.4 constant_dynamic-slice_fusion.3
  558.9 1.4 constant_dynamic-slice_fusion.3
  563.5 1.4 constant_dynamic-slice_fusion.3
  568.2 1.4 constant_dynamic-slice_fusion.3
  572.8 1.4 constant_dynamic-slice_fusion.3
  577.4 1.4 constant_dynamic-slice_fusion.3
  582.0 1.4 constant_dynamic-slice_fusion.3
  586.7 1.4 constant_dynamic-slice_fusion.3
  591.3 1.4 constant_dynamic-slice_fusion.3
  595.9 1.4 constant_dynamic-slice_fusion.3
  598.6 136.7 %all-gather.8.cloned.1.call-done = bf16[256,5120]{0,1:T(8,128)(2,1)} async-done(((bf16[256,160]{0,1:T(8,128)(2,1)}), bf16[256,5120]{0,1:T(8,128)(2,1)}) %all-gather.8.cloned.1.call-update) | async-done | bytes 2621456 | tf_op jit(solution)/shard_map/all_gather | solution.py:101
  735.3 2.9 convolution_convert_fusion
  738.2 3.6 copy.29
  741.9 166.1 %reduce-scatter.4.cloned.1.call-done = bf16[320,320]{1,0:T(8,128)(2,1)} async-done(((bf16[5120,320]{1,0:T(8,128)(2,1)}), bf16[320,320]{1,0:T(8,128)(2,1)}) %reduce-scatter.4.cloned.1.call-update) | async-done | bytes 204816
  907.9 1.1 copy.30
  (186 shorter events, 53.9 us)
Async XLA Ops:
  6.5 36.2 %copy-start.1 = (bf16[320,256]{1,0:T(8,128)(2,1)S(1)}, bf16[320,256]{1,0:T(8,128)(2,1)}, u32[]{:S(2)}) copy-start(bf16[320,256]{1,0:T(8,128)(2,1)} %param.10) | copy-start | bytes 491524
  6.5 36.2 %copy-start.3 = (f32[256]{0:T(256)S(1)}, f32[256]{0:T(256)}, u32[]{:S(2)}) copy-start(f32[256]{0:T(256)} %param.14) | copy-start | bytes 3076
  6.5 257.2 %all-gather.4.cloned.1.call-start = ((), (), s32[]{:S(2)}) async-start(), calls=%async_computation.1 | async-start | bytes 5406720 | tf_op jit(solution)/shard_map/all_gather | solution.py:93
  40.2 465.9 %all-gather.6.cloned.1.call-start = ((), (), s32[]{:S(2)}) async-start(), calls=%async_computation.2 | async-start | bytes 5406720 | tf_op jit(solution)/shard_map/all_gather | solution.py:94
  41.9 693.4 %all-gather.8.cloned.1.call-start = ((), (), s32[]{:S(2)}) async-start(), calls=%async_computation.3 | async-start | bytes 2703360 | tf_op jit(solution)/shard_map/all_gather | solution.py:101
  42.7 865.3 %reduce-scatter.4.cloned.1.call-start = ((), (), s32[]{:S(2)}) async-start(), calls=%async_computation.4 | async-start | bytes 4177920
  598.6 136.7 %copy-start = (f32[2,320,128]{2,1,0:T(8,128)}, f32[2,320,128]{2,1,0:T(8,128)S(1)}, u32[]{:S(2)}) copy-start(f32[2,320,128]{2,1,0:T(8,128)S(1)} %get-tuple-element.53) | copy-start | bytes 983044
  741.9 167.2 %copy-start.2 = (f32[320]{0:T(512)S(1)}, f32[320]{0:T(512)}, u32[]{:S(2)}) copy-start(f32[320]{0:T(512)} %param.16) | copy-start | bytes 3844
Sparse Core Ops, SparseCore 0:
  40.4 223.3 all-gather.3
  265.8 240.2 all-gather.5
  508.3 226.9 all-gather.7
  742.0 165.8 reduce-scatter.3
